TPU v7x, 512 devices: a whole 4x8x8 slice. The times are simulated.
512 devices in a mesh: cfg: 2 (over y_hi), seq: 32 (over z, y_lo), blk: 8 (over x, core).
Axes of the slice: x: 4, y: 8 (y_hi: 2, y_lo: 4; y = y_hi * 4 + y_lo), z: 8, core: 2. Of those that a mesh axis runs over, the one named last changes fastest.
Arguments:
- tokens_in: bfloat16 [2, 4096, 1536], P('cfg', 'seq'), may hold values from -6 to 6
- modulation: float32 [2, 8, 1536], replicated, may hold values from -3 to 3
- qk_gain: float32 [2, 64], replicated, as said below
- qkv_weight: bfloat16 [3, 1536, 1536], P(None, 'blk'), may hold values from -0.15625 to 0.15625
- out_weight: bfloat16 [1536, 1536], P('blk'), may hold values from -0.15625 to 0.15625
- up_weight: bfloat16 [1536, 6144], P('seq', 'blk'), may hold values from -0.15625 to 0.15625
- down_weight: bfloat16 [6144, 1536], P('blk', 'seq'), may hold values from -0.078125 to 0.078125
- proj_weight: bfloat16 [1536, 64], replicated, may hold values from -0.15625 to 0.15625
- latent: float32 [4096, 64], P(('seq', 'blk'), 'cfg'), may hold values from -6 to 6
- text_count: int32 [1], replicated, may hold values from 64 to 2047
- positions: int32 [3, 4096], P(None, 'seq'), may hold values from 0 to 47
- step_index: int32 [1], replicated, may hold values from 20 to 999
- guidance: float32 [1], replicated, may hold values from 4 to 8
Outputs:
- hidden_out: bfloat16 [2, 4096, 1536], P('cfg', ('seq', 'blk'))
- latent_prev: float32 [4096, 64], P(('seq', 'blk'), 'cfg')
Inputs may be any that keep to these rules, and one draw needn't show every extreme that they name: `qk_gain`: positive gains.
All inputs are finite; a program needn't handle non-finite values.
Results may differ from a plain program's by a relative error of at most 0.015.
The roundings to bfloat16 on the way count: a program that leaves them out, or rounds other values in their place, can miss the bound.
Values may be sent and summed in bfloat16 or wider, within the bound.
No kernel may reach another device: no remote copies, remote signals or barrier semaphores. Data moves between devices by JAX's collectives and lax.ppermute only.
A program may use at most 64 MiB of HBM per device.

v0:
```python
import math
import jax
import jax.numpy as jnp
from jax import lax
from jax.sharding import PartitionSpec as P

HEAD = 64
STRIDE = 20
rope_bands = (16, 24, 24)


def swapped(block, axis, stride):
    count = lax.axis_size(axis)
    route = []
    for low in range(count):
        high = low | 1 << stride
        if high != low and high < count:
            route += [(low, high), (high, low)]
    return lax.ppermute(block, axis, route)


def layer_norm(values, epsilon):
    average = jnp.mean(values, -1, keepdims=True)
    centered = values - average
    spread = jnp.mean(centered * centered, -1, keepdims=True)
    return centered * lax.rsqrt(spread + epsilon)


def pick_mods(modulation, is_video, which):
    return jnp.where(
        is_video[:, None], modulation[1, which][None, :], modulation[0, which][None, :]
    )


def modulate(values, modulation, is_video, shift_row, scale_row):
    normed = layer_norm(values, 1e-05)
    return normed * (1.0 + pick_mods(modulation, is_video, scale_row)) + pick_mods(
        modulation, is_video, shift_row
    )


def rope_tables(positions, is_video):
    angle_parts = []
    for axis_pos, band_width in enumerate(rope_bands):
        exponent = jnp.arange(band_width // 2, dtype=jnp.float32) * (2.0 / band_width)
        inverse = jnp.exp(-exponent * math.log(10000.0))
        angle_parts.append(positions[axis_pos].astype(jnp.float32)[:, None] * inverse[None, :])
    angles = jnp.concatenate(angle_parts, 1) * is_video.astype(jnp.float32)[:, None]
    return (jnp.cos(angles), jnp.sin(angles))


def rotate(vectors, cosine, sine):
    pieces = []
    offset = 0
    half_offset = 0
    for band_width in rope_bands:
        half_width = band_width // 2
        first_half = vectors[..., offset : offset + half_width]
        second = vectors[..., offset + half_width : offset + band_width]
        cos_band = cosine[:, None, half_offset : half_offset + half_width]
        sin_band = sine[:, None, half_offset : half_offset + half_width]
        pieces.append(first_half * cos_band - second * sin_band)
        pieces.append(second * cos_band + first_half * sin_band)
        offset = offset + band_width
        half_offset = half_offset + half_width
    return jnp.concatenate(pieces, -1)


def head_prep(flat_heads, gain, cosine, sine):
    token_count = flat_heads.shape[0]
    shaped = flat_heads.reshape(token_count, -1, HEAD)
    normed = layer_norm(shaped, 1e-06) * gain[None, None, :]
    turned = rotate(normed, cosine, sine)
    return turned.reshape(token_count, -1).astype(jnp.bfloat16)


def ddim_update(latent, guided, step_index):
    steps_all = jnp.arange(1000, dtype=jnp.float32)
    root_beta = math.sqrt(0.00085) + steps_all / 999.0 * (math.sqrt(0.012) - math.sqrt(0.00085))
    alpha_bar = jnp.exp(jnp.cumsum(jnp.log1p(-root_beta * root_beta)))
    indices = jnp.arange(1000, dtype=jnp.int32)
    alpha_now = jnp.sum(jnp.where(indices == step_index[0], alpha_bar, 0.0))
    alpha_prev = jnp.sum(jnp.where(indices == step_index[0] - STRIDE, alpha_bar, 0.0))
    clean_est = jnp.sqrt(alpha_now) * latent - jnp.sqrt(1.0 - alpha_now) * guided
    noise_est = jnp.sqrt(1.0 - alpha_now) * latent + jnp.sqrt(alpha_now) * guided
    return jnp.sqrt(alpha_prev) * clean_est + jnp.sqrt(1.0 - alpha_prev) * noise_est


def body(
    tokens_in,
    modulation,
    qk_gain,
    qkv_weight,
    out_weight,
    up_weight,
    down_weight,
    proj_weight,
    latent,
    text_count,
    positions,
    step_index,
    guidance,
):
    row_count = tokens_in.shape[1]
    own_count = row_count // lax.axis_size("blk")
    blk_index = lax.axis_index("blk")
    token_ids = lax.axis_index("seq") * row_count + jnp.arange(row_count, dtype=jnp.int32)
    is_video = token_ids >= text_count[0]
    own_video = lax.dynamic_slice_in_dim(is_video, blk_index * own_count, own_count, 0)
    residual = tokens_in[0].astype(jnp.float32)
    cosine, sine = rope_tables(positions, is_video)
    normed = modulate(residual, modulation, is_video, 0, 1).astype(jnp.bfloat16)
    projected = jnp.einsum("td,ked->kte", normed, qkv_weight, preferred_element_type=jnp.float32)
    head_count = projected.shape[2] // HEAD
    queries = head_prep(projected[0], qk_gain[0], cosine, sine)
    keys_local = head_prep(projected[1], qk_gain[1], cosine, sine)
    values_local = projected[2].astype(jnp.bfloat16)
    query_heads = queries.reshape(row_count, head_count, HEAD)
    initial = (
        jnp.full((head_count, row_count), -1e30, jnp.float32),
        jnp.zeros((head_count, row_count), jnp.float32),
        jnp.zeros((head_count, row_count, HEAD), jnp.float32),
    )
    key_piece = lax.all_gather(keys_local, "seq", axis=0, tiled=True)
    value_piece = lax.all_gather(values_local, "seq", axis=0, tiled=True)
    piece_len = key_piece.shape[0]
    key_blocks = key_piece.reshape(piece_len // piece_len, piece_len, head_count, HEAD)
    value_blocks = value_piece.reshape(piece_len // piece_len, piece_len, head_count, HEAD)

    def absorb_block(state, key_value):
        key_block, value_block = key_value
        running_max, running_sum, weighted = state
        scores = (
            jnp.einsum("thd,shd->hts", query_heads, key_block, preferred_element_type=jnp.float32)
            * 0.125
        )
        new_max = jnp.maximum(running_max, jnp.max(scores, -1))
        rescale = jnp.exp(running_max - new_max)
        weights = jnp.exp(scores - new_max[..., None])
        running_sum = running_sum * rescale + jnp.sum(weights, -1)
        weighted = weighted * rescale[..., None] + jnp.einsum(
            "hts,shd->htd",
            weights.astype(jnp.bfloat16),
            value_block,
            preferred_element_type=jnp.float32,
        )
        return ((new_max, running_sum, weighted), None)

    state, unused = lax.scan(absorb_block, initial, (key_blocks, value_blocks))
    running_max, running_sum, weighted = state
    attn_out = (
        (weighted / running_sum[..., None])
        .transpose(1, 0, 2)
        .reshape(row_count, head_count * HEAD)
        .astype(jnp.bfloat16)
    )
    attn_proj = lax.psum(
        jnp.dot(attn_out, out_weight, preferred_element_type=jnp.float32).astype(jnp.bfloat16),
        "blk",
    ).astype(jnp.float32)
    after_attn = residual + pick_mods(modulation, is_video, 2) * attn_proj
    normed_mlp = modulate(after_attn, modulation, is_video, 3, 4).astype(jnp.bfloat16)
    own_after = lax.dynamic_slice_in_dim(after_attn, blk_index * own_count, own_count, 0)
    up_full, down_full = (
        lax.all_gather(up_weight, "seq", axis=0, tiled=True),
        lax.all_gather(down_weight, "seq", axis=1, tiled=True),
    )
    hidden_up = jnp.dot(normed_mlp, up_full, preferred_element_type=jnp.float32)
    activated = jax.nn.gelu(hidden_up, approximate=True).astype(jnp.bfloat16)
    mlp_part = jnp.dot(activated, down_full, preferred_element_type=jnp.float32)
    mlp_rows = lax.psum_scatter(
        mlp_part.astype(jnp.bfloat16), "blk", scatter_dimension=0, tiled=True
    ).astype(jnp.float32)
    after_mlp = own_after + pick_mods(modulation, own_video, 5) * mlp_rows
    hidden_out = after_mlp.astype(jnp.bfloat16)[None]
    final_norm = modulate(after_mlp, modulation, own_video, 6, 7).astype(jnp.bfloat16)
    predicted = jnp.dot(final_norm, proj_weight, preferred_element_type=jnp.float32)
    half_width = latent.shape[1]
    branch_index = lax.axis_index("cfg")
    kept = lax.dynamic_slice_in_dim(predicted, branch_index * half_width, half_width, 1)
    outgoing = lax.dynamic_slice_in_dim(predicted, (1 - branch_index) * half_width, half_width, 1)
    partner = swapped(outgoing, "cfg", 0)
    is_cond = branch_index == 0
    cond_pred = jnp.where(is_cond, kept, partner)
    uncond_pred = jnp.where(is_cond, partner, kept)
    guided = uncond_pred + guidance[0] * (cond_pred - uncond_pred)
    latent_prev = ddim_update(latent, guided, step_index)
    return (hidden_out, latent_prev)


def solution(mesh):
    in_specs = (
        P("cfg", "seq", None),
        P(),
        P(),
        P(None, "blk", None),
        P("blk", None),
        P("seq", "blk"),
        P("blk", "seq"),
        P(),
        P(("seq", "blk"), "cfg"),
        P(),
        P(None, "seq"),
        P(),
        P(),
    )
    out_specs = (P("cfg", ("seq", "blk"), None), P(("seq", "blk"), "cfg"))
    return jax.shard_map(body, mesh=mesh, in_specs=in_specs, out_specs=out_specs, check_vma=False)
```

profile of v0, /device:TPU:64, one launch (start us, length us, event | category | flops | bytes accessed | tf_op | source)
XLA Modules:
  0.0 744.4 jit_solution(7766577091344267166)
XLA Ops:
  8.0 0.8 convert_bitcast_fusion.4
  9.1 1.8 slice_reduce_fusion.3
  10.9 1.1 convert_reduce_fusion
  12.0 1.3 fusion.21
  13.3 1.7 convolution_bitcast_fusion
  15.4 5.1 concatenate.13
  20.6 0.6 slice.262
  21.4 0.3 concatenate.12
  21.7 134.0 %all-gather.6.cloned.1.call-done = bf16[4096,192]{0,1:T(8,128)(2,1)} async-done(((bf16[128,192]{0,1:T(8,128)(2,1)}), bf16[4096,192]{0,1:T(8,128)(2,1)}) %all-gather.6.cloned.1.call-update) | async-done | bytes 1572880 | tf_op jit(solution)/shard_map/all_gather | solution.py:124
  155.6 2.5 fusion.90
  158.2 1.0 fusion
  159.1 1.7 copy-done.1
  160.8 124.8 %all-gather.12.cloned.1.call-done = bf16[1,4096,192]{1,2,0:T(8,128)(2,1)} async-done(((bf16[1,128,192]{1,2,0:T(8,128)(2,1)}), bf16[1,4096,192]{1,2,0:T(8,128)(2,1)}) %all-gather.12.cloned.1.call-update) | async-done | bytes 1572880 | tf_op jit(solution)/shard_map/all_gather | solution.py:125
  285.6 4.6 fusion.14
  290.3 1.1 convolution_convert_fusion.1
  291.4 0.5 all-gather.10.cloned.1.call-update
  292.0 0.5 all-gather.8.cloned.1.call-update
  292.6 66.6 %all-reduce.3.cloned.1.call-done = bf16[128,1536]{1,0:T(8,128)(2,1)} async-done(((bf16[128,1536]{1,0:T(8,128)(2,1)}), bf16[128,1536]{1,0:T(8,128)(2,1)}) %all-reduce.3.cloned.1.call-update) | async-done | bytes 393232 | tf_op jit(solution)/shard_map/psum | solution.py:157
  359.1 1.3 fusion.84
  360.4 0.2 multiply_reduce_fusion
  360.7 154.4 %all-gather.10.cloned.1.call-done = bf16[768,1536]{0,1:T(8,128)(2,1)} async-done(((bf16[768,48]{0,1:T(8,128)(2,1)}), bf16[768,1536]{0,1:T(8,128)(2,1)}) %all-gather.10.cloned.1.call-update) | async-done | bytes 2359312 | tf_op jit(solution)/shard_map/all_gather | solution.py:166
  515.1 162.1 %all-gather.8.cloned.1.call-done = bf16[1536,768]{1,0:T(8,128)(2,1)} async-done(((bf16[48,768]{1,0:T(8,128)(2,1)}), bf16[1536,768]{1,0:T(8,128)(2,1)}) %all-gather.8.cloned.1.call-update) | async-done | bytes 2359312 | tf_op jit(solution)/shard_map/all_gather | solution.py:165
  677.3 4.5 convolution_convert_fusion
  681.9 0.3 reduce-window.9
  683.0 0.1 slice_reduce_fusion.16
  683.1 40.3 %reduce-scatter.2.cloned.1.call-done = bf16[16,1536]{1,0:T(8,128)(2,1)} async-done(((bf16[128,1536]{1,0:T(8,128)(2,1)}), bf16[16,1536]{1,0:T(8,128)(2,1)}) %reduce-scatter.2.cloned.1.call-update) | async-done | bytes 49168 | tf_op jit(solution)/shard_map/reduce_scatter | solution.py:171
  723.4 1.0 fusion.83
  724.4 0.7 multiply_reduce_fusion.1
  725.2 0.2 fusion.64
  725.5 7.4 collective-permute-start
  732.9 0.7 select_reduce_fusion
  736.9 0.7 multiply_add_fusion.1
  (62 shorter events, 1.4 us)
Async XLA Ops:
  7.2 6.2 copy-start
  7.2 148.4 %all-gather.6.cloned.1.call-start = ((), (), s32[]{:S(2)}) async-start(), calls=%async_computation.1 | async-start | bytes 1622016 | tf_op jit(solution)/shard_map/all_gather | solution.py:124
  12.0 3.2 copy-start.5
  20.5 265.1 %all-gather.12.cloned.1.call-start = ((), (), s32[]{:S(2)}) async-start(), calls=%async_computation.6 | async-start | bytes 1622016 | tf_op jit(solution)/shard_map/all_gather | solution.py:125
  21.3 337.8 %all-reduce.3.cloned.1.call-start = ((), (), s32[]{:S(2)}) async-start(), calls=%async_computation.2 | async-start | bytes 786432 | tf_op jit(solution)/shard_map/psum | solution.py:157
  158.1 2.7 copy-start.1
  285.6 4.6 copy-start.3
  285.6 73.5 %copy-start.2 = (bf16[1,128,1536]{2,1,0:T(8,128)(2,1)S(1)}, bf16[1,128,1536]{2,1,0:T(8,128)(2,1)}, u32[]{:S(2)}) copy-start(bf16[1,128,1536]{2,1,0:T(8,128)(2,1)} %param.13) | copy-start | bytes 1179652
  291.3 223.8 %all-gather.10.cloned.1.call-start = ((), (), s32[]{:S(2)}) async-start(), calls=%async_computation.4 | async-start | bytes 2433024 | tf_op jit(solution)/shard_map/all_gather | solution.py:166
  291.9 385.3 %all-gather.8.cloned.1.call-start = ((), (), s32[]{:S(2)}) async-start(), calls=%async_computation.3 | async-start | bytes 2433024 | tf_op jit(solution)/shard_map/all_gather | solution.py:165
  292.5 430.9 %reduce-scatter.2.cloned.1.call-start = ((), (), s32[]{:S(2)}) async-start(), calls=%async_computation.5 | async-start | bytes 442368 | tf_op jit(solution)/shard_map/reduce_scatter | solution.py:171
  677.3 47.9 %copy-start.6 = (bf16[1536,64]{0,1:T(8,128)(2,1)S(1)}, bf16[1536,64]{0,1:T(8,128)(2,1)}, u32[]{:S(2)}) copy-start(bf16[1536,64]{0,1:T(8,128)(2,1)} %param.20) | copy-start | bytes 589828
  677.3 59.6 %copy-start.4 = (f32[16,32]{1,0:T(8,128)S(1)}, f32[16,32]{1,0:T(8,128)}, u32[]{:S(2)}) copy-start(f32[16,32]{1,0:T(8,128)} %param.21) | copy-start | bytes 6148
  725.5 11.4 %collective-permute-start = (f32[16,32]{1,0:T(8,128)S(1)}, f32[16,32]{1,0:T(8,128)S(1)}, u32[]{:S(2)}, u32[]{:S(2)}) collective-permute-start(f32[16,32]{1,0:T(8,128)S(1)} %constant_dynamic-slice_fusion), channel_id=1, source_target_pairs={{0,256},{256,0},{1,257},{257,1},{2,258},{258,2},{3,259},{259,3},{4... | collective-permute-start | bytes 6152 | tf_op jit(solution)/shard_map/ppermute | solution.py:19
Sparse Core Ops, SparseCore 0:
  20.7 134.9 all-gather.5
  158.2 127.3 all-gather.11
  291.5 67.6 all-reduce.2
  361.3 153.8 all-gather.9
  517.2 159.9 all-gather.7
  681.9 41.4 reduce-scatter.1
where the time goes:
time: 745 us; the launch traced here: 744 us
  waiting for transfers between devices  683 us (92%)
  between operations  19.1 us (3%)
  matrix products  14.7 us (2%)
  local copies, waits for them, and re-layouts  9.89 us (1%)
  other arithmetic  9.82 us (1%)
  starting transfers between devices  7.61 us (1%)
    all_gather x1, waiting for transfers between devices, body(): lax.all_gather(up_weight, 'seq', axis=0, tiled=True)  162 us
    all_gather x1, waiting for transfers between devices, body(): lax.all_gather(down_weight, 'seq', axis=1, tiled=True)  154 us
    all_gather x1, waiting for transfers between devices, body(): key_piece = lax.all_gather(keys_local, 'seq', axis=0, tiled=True)  134 us
    all_gather x1, waiting for transfers between devices, body(): value_piece = lax.all_gather(values_local, 'seq', axis=0, tiled=True)  125 us
    psum x1, waiting for transfers between devices, body(): lax.psum(jnp.dot(attn_out, out_weight, preferred_element_type=jnp.float32...  66.6 us
    reduce_scatter x1, waiting for transfers between devices, body(): lax.psum_scatter(mlp_part.astype(jnp.bfloat16), 'blk', scatter_dimension=...  40.3 us
  transfers between devices with their start and end apart: 7, of which 6 were waited for; matrix products, arithmetic and copies ran while one was open for 1% of the time, Pallas kernels for 0%

commit v1 on v0

--- a/solution.py
+++ b/solution.py
@@ -121,8 +121,13 @@
         jnp.zeros((head_count, row_count), jnp.float32),
         jnp.zeros((head_count, row_count, HEAD), jnp.float32),
     )
-    key_piece = lax.all_gather(keys_local, "seq", axis=0, tiled=True)
-    value_piece = lax.all_gather(values_local, "seq", axis=0, tiled=True)
+    key_piece, value_piece = jnp.split(
+        lax.all_gather(
+            jnp.concatenate([keys_local, values_local], axis=1), "seq", axis=0, tiled=True
+        ),
+        [keys_local.shape[1]],
+        axis=1,
+    )
     piece_len = key_piece.shape[0]
     key_blocks = key_piece.reshape(piece_len // piece_len, piece_len, head_count, HEAD)
     value_blocks = value_piece.reshape(piece_len // piece_len, piece_len, head_count, HEAD)

time: 745 us -> 633 us (0.85)
  waiting for transfers between devices: 683 us -> 581 us
    all_gather x2 -> x1, waiting for transfers between devices: 259 us -> 153 us  [body(): lax.all_gather(jnp.concatenate([keys_local, values_local], axis=1), 'seq'...]
    all_gather x1, waiting for transfers between devices: 154 us -> 162 us  [body(): lax.all_gather(down_weight, 'seq', axis=1, tiled=True)]
    all_gather x1, waiting for transfers between devices: 162 us -> 155 us  [body(): lax.all_gather(up_weight, 'seq', axis=0, tiled=True)]
  transfers between devices with their start and end apart: 7 -> 6, of which waited for: 6 -> 5; matrix products, arithmetic and copies ran while one was open for 1% -> 1% of each run, Pallas kernels for 0% -> 0%
where the time goes in v1:
time: 633 us
  waiting for transfers between devices  581 us (92%)
  between operations  18.8 us (3%)
  other arithmetic  10.5 us (2%)
  matrix products  9.96 us (2%)
  starting transfers between devices  7.55 us (1%)
    all_gather x1, waiting for transfers between devices, body(): lax.all_gather(down_weight, 'seq', axis=1, tiled=True)  162 us
    all_gather x1, waiting for transfers between devices, body(): lax.all_gather(up_weight, 'seq', axis=0, tiled=True)  155 us
    all_gather x1, waiting for transfers between devices, body(): lax.all_gather(jnp.concatenate([keys_local, values_local], axis=1), 'seq'...  153 us
    psum x1, waiting for transfers between devices, body(): lax.psum(jnp.dot(attn_out, out_weight, preferred_element_type=jnp.float32...  69.7 us
    reduce_scatter x1, waiting for transfers between devices, body(): lax.psum_scatter(mlp_part.astype(jnp.bfloat16), 'blk', scatter_dimension=...  40.3 us
  transfers between devices with their start and end apart: 6, of which 5 were waited for; matrix products, arithmetic and copies ran while one was open for 1% of the time, Pallas kernels for 0%

profile of v1, /device:TPU:64, one launch (start us, length us, event | category | flops | bytes accessed | tf_op | source)
XLA Modules:
  0.0 632.6 jit_solution(8798381422917297071)
XLA Ops:
  8.0 0.8 convert_bitcast_fusion.4
  9.1 1.8 slice_reduce_fusion.3
  10.9 1.1 convert_reduce_fusion
  12.0 1.2 fusion.21
  13.3 1.7 convolution_bitcast_fusion
  15.3 0.1 multiply_multiply_fusion.1
  15.4 0.3 concatenate.16
  15.7 0.6 pad_maximum_fusion
  16.5 0.3 concatenate.15
  16.8 153.0 %all-gather.4.cloned.1.call-done = bf16[4096,384]{0,1:T(8,128)(2,1)} async-done(((bf16[128,384]{0,1:T(8,128)(2,1)}), bf16[4096,384]{0,1:T(8,128)(2,1)}) %all-gather.4.cloned.1.call-update) | async-done | bytes 3145744 | tf_op jit(solution)/shard_map/all_gather | solution.py:125
  169.8 2.2 fusion.88
  171.9 1.1 fusion.92
  173.0 1.0 fusion
  174.1 1.3 fusion.14
  175.4 1.1 convolution_convert_fusion.1
  176.5 0.7 all-gather.6.cloned.1.call-update
  177.3 0.5 all-gather.8.cloned.1.call-update
  177.8 69.7 %all-reduce.3.cloned.1.call-done = bf16[128,1536]{1,0:T(8,128)(2,1)} async-done(((bf16[128,1536]{1,0:T(8,128)(2,1)}), bf16[128,1536]{1,0:T(8,128)(2,1)}) %all-reduce.3.cloned.1.call-update) | async-done | bytes 393232 | tf_op jit(solution)/shard_map/psum | solution.py:162
  247.5 1.3 fusion.85
  248.8 0.2 multiply_reduce_fusion
  249.1 154.6 %all-gather.6.cloned.1.call-done = bf16[1536,768]{1,0:T(8,128)(2,1)} async-done(((bf16[48,768]{1,0:T(8,128)(2,1)}), bf16[1536,768]{1,0:T(8,128)(2,1)}) %all-gather.6.cloned.1.call-update) | async-done | bytes 2359312 | tf_op jit(solution)/shard_map/all_gather | solution.py:170
  403.7 162.1 %all-gather.8.cloned.1.call-done = bf16[768,1536]{0,1:T(8,128)(2,1)} async-done(((bf16[768,48]{0,1:T(8,128)(2,1)}), bf16[768,1536]{0,1:T(8,128)(2,1)}) %all-gather.8.cloned.1.call-update) | async-done | bytes 2359312 | tf_op jit(solution)/shard_map/all_gather | solution.py:171
  565.8 4.5 convolution_convert_fusion
  570.5 0.3 reduce-window.9
  571.5 0.1 slice_reduce_fusion.16
  571.7 40.3 %reduce-scatter.2.cloned.1.call-done = bf16[16,1536]{1,0:T(8,128)(2,1)} async-done(((bf16[128,1536]{1,0:T(8,128)(2,1)}), bf16[16,1536]{1,0:T(8,128)(2,1)}) %reduce-scatter.2.cloned.1.call-update) | async-done | bytes 49168 | tf_op jit(solution)/shard_map/reduce_scatter | solution.py:176
  612.0 1.0 fusion.84
  613.0 0.7 multiply_reduce_fusion.1
  613.7 0.2 fusion.64
  614.0 7.4 %collective-permute-start = (f32[16,32]{1,0:T(8,128)S(1)}, f32[16,32]{1,0:T(8,128)S(1)}, u32[]{:S(2)}, u32[]{:S(2)}) collective-permute-start(f32[16,32]{1,0:T(8,128)S(1)} %constant_dynamic-slice_fusion), channel_id=1, source_target_pairs={{0,256},{256,0},{1,257},{257,1},{2,258},{258,2},{3,259},{259,3},{4... | collective-permute-start | bytes 6152 | tf_op jit(solution)/shard_map/ppermute | solution.py:19
  621.4 0.7 select_reduce_fusion
  625.4 0.7 multiply_add_fusion.1
  (59 shorter events, 1.2 us)
Async XLA Ops:
  7.2 6.1 copy-start
  7.2 162.6 %all-gather.4.cloned.1.call-start = ((), (), s32[]{:S(2)}) async-start(), calls=%async_computation.1 | async-start | bytes 3244032 | tf_op jit(solution)/shard_map/all_gather | solution.py:125
  13.3 2.0 copy-start.4
  16.4 231.1 %all-reduce.3.cloned.1.call-start = ((), (), s32[]{:S(2)}) async-start(), calls=%async_computation.2 | async-start | bytes 786432 | tf_op jit(solution)/shard_map/psum | solution.py:162
  174.1 1.3 copy-start.2
  174.1 73.5 %copy-start.1 = (bf16[1,128,1536]{2,1,0:T(8,128)(2,1)S(1)}, bf16[1,128,1536]{2,1,0:T(8,128)(2,1)}, u32[]{:S(2)}) copy-start(bf16[1,128,1536]{2,1,0:T(8,128)(2,1)} %param.13) | copy-start | bytes 1179652
  176.5 227.2 %all-gather.6.cloned.1.call-start = ((), (), s32[]{:S(2)}) async-start(), calls=%async_computation.3 | async-start | bytes 2433024 | tf_op jit(solution)/shard_map/all_gather | solution.py:170
  177.2 388.6 %all-gather.8.cloned.1.call-start = ((), (), s32[]{:S(2)}) async-start(), calls=%async_computation.4 | async-start | bytes 2433024 | tf_op jit(solution)/shard_map/all_gather | solution.py:171
  177.8 434.2 %reduce-scatter.2.cloned.1.call-start = ((), (), s32[]{:S(2)}) async-start(), calls=%async_computation.5 | async-start | bytes 442368 | tf_op jit(solution)/shard_map/reduce_scatter | solution.py:176
  565.8 47.9 %copy-start.5 = (bf16[1536,64]{0,1:T(8,128)(2,1)S(1)}, bf16[1536,64]{0,1:T(8,128)(2,1)}, u32[]{:S(2)}) copy-start(bf16[1536,64]{0,1:T(8,128)(2,1)} %param.20) | copy-start | bytes 589828
  565.8 59.6 %copy-start.3 = (f32[16,32]{1,0:T(8,128)S(1)}, f32[16,32]{1,0:T(8,128)}, u32[]{:S(2)}) copy-start(f32[16,32]{1,0:T(8,128)} %param.21) | copy-start | bytes 6148
  614.0 11.4 %collective-permute-start = (f32[16,32]{1,0:T(8,128)S(1)}, f32[16,32]{1,0:T(8,128)S(1)}, u32[]{:S(2)}, u32[]{:S(2)}) collective-permute-start(f32[16,32]{1,0:T(8,128)S(1)} %constant_dynamic-slice_fusion), channel_id=1, source_target_pairs={{0,256},{256,0},{1,257},{257,1},{2,258},{258,2},{3,259},{259,3},{4... | collective-permute-start | bytes 6152 | tf_op jit(solution)/shard_map/ppermute | solution.py:19
Sparse Core Ops, SparseCore 0:
  16.5 153.1 all-gather.3
  176.6 70.8 all-reduce.2
  249.8 153.8 all-gather.5
  405.8 159.9 all-gather.7
  570.5 41.4 reduce-scatter.1
